TPU v7x, 32 devices: a whole 2x2x4 slice. The times are simulated.
32 devices in a mesh: groups: 2 (over x), ctx: 4 (over y, core), head: 4 (over z).
Axes of the slice: x: 2, y: 2, z: 4, core: 2. Of those that a mesh axis runs over, the one named last changes fastest.
Arguments:
- xs: bfloat16 [12288, 4096], P(('groups', 'ctx', 'head')), parts along dimension 0, may hold values from -6 to 6
- gate_in: bfloat16 [12288, 4096], P(('groups', 'ctx', 'head')), parts along dimension 0, may hold values from -6 to 6
- bc: bfloat16 [12288, 256], P(('groups', 'ctx', 'head')), parts along dimension 0, may hold values from -1.78125 to 1.78125
- dt_raw: bfloat16 [12288, 64], P(('groups', 'ctx', 'head')), parts along dimension 0, may hold values from -4 to 4
- doc_ids: int32 [12288], P(('groups', 'ctx')), parts along dimension 0, may hold values from 0 to 31, never falling along the last dimension, each value on 1 to 3072 neighbouring positions
- dt_bias: float32 [64], P('head'), may hold values from -1 to 1
- decay_rate: float32 [64], P('head'), may hold values from 8.138021e-06 to 0.03
- skip: float32 [64], P('head'), may hold values from 0.5 to 1.5
- norm_gain: float32 [4096], replicated, may hold values from 0.5 to 1.5
Outputs:
- mixed: bfloat16 [12288, 4096], P(('groups', 'ctx', 'head')), parts along dimension 0
There are 2 independent parts, one for each index of `groups`. A program takes and returns all parts, laid end to end along the dimension named above; an argument that names none is the same for every part. Nothing has to cross between parts.
Inputs may be any that keep to these rules, and one draw needn't show every extreme that they name: `doc_ids`: document ids never fall along the window; each document is one run of tokens, at most 3072 long, and one document is exactly that long.
All inputs are finite; a program needn't handle non-finite values.
Results may differ from a plain program's by a relative error of at most 0.007.
Values may be sent and summed in bfloat16 or wider, within the bound.
A program may use at most 64 MiB of HBM per device.

v0:
```python
import jax
import jax.numpy as jnp
from jax import lax
from jax.sharding import PartitionSpec as P

HDIM = 64
STATE = 128
STRETCH = 256


def from_behind(array, axis, by):
    size = lax.axis_size(axis)
    pairs = [(i, i + by) for i in range(size) if 0 <= i + by < size]
    return lax.ppermute(array, axis, pairs)


def join_states(earlier, later):
    early_front, early_back, early_mult, early_state = earlier
    late_front, late_back, late_mult, late_state = later
    early_none = early_back < 0.5
    late_none = late_front < 0.5
    linked = jnp.where((late_front == early_back) | early_none | late_none, 1.0, 0.0).astype(
        jnp.float32
    )
    front_id = jnp.where(early_none, late_front, early_front)
    back_id = jnp.where(late_none, early_back, late_back)
    factor = late_mult * linked
    return (
        front_id,
        back_id,
        factor * early_mult,
        factor[:, None, None] * early_state + late_state,
    )


def run_blocks(start, multipliers, block_states):

    def advance(carry, pieces):
        mult_block, state_block = pieces
        return (mult_block[:, None, None] * carry + state_block, carry)

    final_state, starts = lax.scan(advance, start, (multipliers, block_states))
    return (starts, final_state)


def apply_states(c_rows, states):
    state_hi = states.astype(jnp.bfloat16)
    state_lo = (states - state_hi.astype(jnp.float32)).astype(jnp.bfloat16)
    first = jnp.einsum("ktn,khpn->kthp", c_rows, state_hi, preferred_element_type=jnp.float32)
    second = jnp.einsum("ktn,khpn->kthp", c_rows, state_lo, preferred_element_type=jnp.float32)
    return first + second


def shards(xs, gate_in, bc, dt_raw, doc_ids, dt_bias, decay_rate, skip, norm_gain):
    head_feats, head_steps = (
        lax.all_to_all(xs, "head", split_axis=1, concat_axis=0, tiled=True),
        lax.all_to_all(dt_raw, "head", split_axis=1, concat_axis=0, tiled=True),
    )
    maps_all = lax.all_gather(bc, "head", axis=0, tiled=True)
    span_tokens = head_feats.shape[0]
    local_heads = head_steps.shape[1]
    blocks = span_tokens // STRETCH
    head_x = head_feats.reshape(blocks, STRETCH, local_heads, HDIM)
    in_b = maps_all[:, :STATE].reshape(blocks, STRETCH, STATE)
    in_c = maps_all[:, STATE:].reshape(blocks, STRETCH, STATE)
    step_size = jax.nn.softplus(head_steps.astype(jnp.float32) + dt_bias[None, :]).reshape(
        blocks, STRETCH, local_heads
    )
    log_decay = jnp.cumsum(-decay_rate[None, None, :] * step_size, axis=1)
    ids = doc_ids.reshape(blocks, STRETCH)
    span_front = doc_ids[0]
    span_back = doc_ids[-1]
    before = jnp.concatenate([span_front[None], ids[:-1, -1]])
    scores = jnp.einsum("ktn,ksn->kts", in_c, in_b, preferred_element_type=jnp.float32)
    lower = jnp.arange(STRETCH)[:, None] >= jnp.arange(STRETCH)[None, :]
    allowed = lower[None, :, :] & (ids[:, :, None] == ids[:, None, :])
    spread = log_decay[:, :, None, :] - log_decay[:, None, :, :]
    decayed = jnp.exp(jnp.where(allowed[:, :, :, None], spread, -jnp.inf))
    mixing = (scores[:, :, :, None] * decayed * step_size[:, None, :, :]).astype(jnp.bfloat16)
    local_y = jnp.einsum("ktsh,kshp->kthp", mixing, head_x, preferred_element_type=jnp.float32)
    last_ids = ids[:, -1]
    log_end = log_decay[:, -1, :]
    factor = jnp.where(
        (ids == last_ids[:, None])[:, :, None],
        jnp.exp(log_end[:, None, :] - log_decay) * step_size,
        0.0,
    )
    weighted = (factor[:, :, :, None] * head_x.astype(jnp.float32)).astype(jnp.bfloat16)
    block_states = jnp.einsum("kshp,ksn->khpn", weighted, in_b, preferred_element_type=jnp.float32)
    keep = jnp.where(last_ids == before, 1.0, 0.0).astype(jnp.float32)
    multipliers = keep[:, None] * jnp.exp(log_end)
    inside_scale = jnp.where((ids == before[:, None])[:, :, None], jnp.exp(log_decay), 0.0)
    zero_state = jnp.zeros((local_heads, HDIM, STATE), jnp.float32)
    local_starts, local_final = run_blocks(zero_state, multipliers, block_states)
    element = (
        (span_front + 1).astype(jnp.float32),
        (span_back + 1).astype(jnp.float32),
        jnp.prod(multipliers, axis=0),
        local_final,
    )
    empty = (jnp.float32(0.0), jnp.float32(0.0), jnp.zeros((local_heads,), jnp.float32), zero_state)

    def hop(step_index, incoming):
        return from_behind(join_states(incoming, element), "ctx", 1)

    arrived = lax.fori_loop(0, lax.axis_size("ctx") - 1, hop, empty)
    matches = jnp.where((arrived[1] == element[0]) & (arrived[1] > 0.5), 1.0, 0.0).astype(
        jnp.float32
    )
    incoming_state = matches * arrived[3]
    starts, unused = run_blocks(incoming_state, multipliers, block_states)
    carried_y = inside_scale[:, :, :, None] * apply_states(in_c, starts)
    ssm_out = local_y + carried_y + skip[None, None, :, None] * head_x.astype(jnp.float32)
    ssm_out = ssm_out.astype(jnp.bfloat16).reshape(span_tokens, local_heads * HDIM)
    token_rows = lax.all_to_all(ssm_out, "head", split_axis=0, concat_axis=1, tiled=True)
    gated = token_rows.astype(jnp.float32) * jax.nn.silu(gate_in.astype(jnp.float32))
    scale = lax.rsqrt(jnp.mean(gated * gated, axis=-1, keepdims=True) + 1e-05)
    return (gated * scale * norm_gain[None, :]).astype(jnp.bfloat16)


def solution(mesh):
    return jax.shard_map(
        shards,
        mesh=mesh,
        in_specs=(
            P(("groups", "ctx", "head"), None),
            P(("groups", "ctx", "head"), None),
            P(("groups", "ctx", "head"), None),
            P(("groups", "ctx", "head"), None),
            P(("groups", "ctx")),
            P("head"),
            P("head"),
            P("head"),
            P(),
        ),
        out_specs=P(("groups", "ctx", "head"), None),
        check_vma=False,
    )
```

profile of v0, /device:TPU:5, one launch (start us, length us, event | category | flops | bytes accessed | tf_op | source)
XLA Modules:
  0.0 288.6 jit_solution(14034544817957534413)
XLA Ops:
  0.0 4.6 %all-to-all-start = ((bf16[384,4,16]{0,2,1:T(8,128)(2,1)}), bf16[384,4,16]{0,2,1:T(8,128)(2,1)S(1)}, u32[]{:S(2)}, u32[]{:S(2)}) async-start(bf16[384,4,16]{0,2,1:T(8,128)(2,1)} %bitcast.87), calls=%async_computation | async-start | bytes 98304 | tf_op jit(solution)/shard_map/all_to_all | solution.py:57
  4.6 4.6 %copy.82 = bf16[384,4096]{0,1:T(8,128)(2,1)} copy(bf16[384,4096]{1,0:T(8,128)(2,1)} %param.15) | data formatting | bytes 6291456 | tf_op args[0]
  9.2 4.8 %all-to-all-start.1 = ((bf16[384,4,1024]{0,2,1:T(8,128)(2,1)}), bf16[384,4,1024]{0,2,1:T(8,128)(2,1)}, u32[]{:S(2)}, u32[]{:S(2)}) async-start(bf16[384,4,1024]{0,2,1:T(8,128)(2,1)} %bitcast.9), calls=%async_computation.1 | async-start | bytes 6291456 | tf_op jit(solution)/shard_map/all_to_all | solution.py:56
  19.2 76.2 %all_gather.3 = bf16[1536,256]{1,0:T(8,128)(2,1)S(1)} all-gather(bf16[384,256]{1,0:T(8,128)(2,1)S(1)} %copy-done.7), channel_id=1, replica_groups=mesh['groups'=2,'ctx'=4,'head'=4] {'head'}, dimensions={0}, use_global_device_ids=true | all-gather | bytes 983040 | tf_op jit(solution)/shard_map/all_gather | solution.py:59
  96.9 3.4 %reduce-window.6 = f32[6,16,2,128]{3,1,2,0:T(8,128)S(1)} reduce-window(f32[6,16,2,128]{3,1,2,0:T(8,128)S(1)} %copy.76, f32[]{:T(128)} %constant.55.clone.1), window={size=1x1x1x128 pad=0_0x0_0x0_0x127_0}, to_apply=%region_0.1 | reduce-window | flops 3121152 | bytes 196612 | tf_op jit(solution)/shard_map/reduce-window
  103.5 6.0 %copy.83 = bf16[4,384,1024]{1,0,2:T(4,128)(2,1)} copy(bf16[4,384,1024]{1,2,0:T(8,128)(2,1)} %bitcast.10) | data formatting | bytes 6291456 | tf_op jit(solution)/shard_map/all_to_all | solution.py:56
  109.5 7.5 %reshape.157 = bf16[6,256,16,64]{1,0,3,2:T(8,128)(2,1)} reshape(bf16[4,384,1024]{1,0,2:T(4,128)(2,1)} %copy.83) | data formatting | bytes 6291456 | tf_op jit(solution)/shard_map/reshape | solution.py:63
  117.0 4.8 %fusion.16 = f32[6,16,64,128]{3,2,1,0:T(8,128)} fusion(bf16[6,256,128,1]{2,1,3,0:T(8,128)(2,1)S(1)} %bitcast.86, f32[6,256,16]{1,2,0:T(8,128)S(1)} %copy.88, bf16[6,256,16,64]{1,0,3,2:T(8,128)(2,1)} %reshape.157), kind=kOutput, calls=%fused_computation.32 | convolution fusion | flops 407371776 | bytes 6782976 | tf_op jit(solution)/shard_map/kshp,ksn->khpn/dot_general | solution.py:89
  121.8 7.2 %while.38 = (s32[]{:T(128)}, f32[16,64,128]{2,1,0:T(8,128)S(1)}, f32[6,16]{1,0:T(8,128)S(1)}, f32[6,16,64,128]{3,2,1,0:T(8,128)}, s32[]{:T(128)}, /*index=5*/s32[]{:T(128)}) while((s32[]{:T(128)}, f32[16,64,128]{2,1,0:T(8,128)S(1)}, f32[6,16]{1,0:T(8,128)S(1)}, f32[6,16,64,128]{3,2,1,0:T(8,128)}, s32[]{:T(128)}, ...), condition=%wide.region_4.5_spmd.clone, body=%wide.region_3.4_spmd.clone.sunk | while | flops 393219 | bytes 1573143 | solution.py:42
  129.0 31.8 %while.36 = (s32[]{:T(128)}, f32[]{:T(128)}, f32[16,64,128]{2,1,0:T(8,128)S(1)}, pred[]{:T(512)}, f32[]{:T(128)}, /*index=5*/f32[]{:T(128)}, f32[16]{0:T(128)S(1...) while((s32[]{:T(128)}, f32[]{:T(128)}, ...), condition=%wide.region_6.7_spmd, body=%wide.region_5.6_spmd.sunk | while | flops 262168 | bytes 3670475 | solution.py:106
  129.2 1.3 collective-permute-start.1
  130.5 1.3 collective-permute-start
  131.8 5.7 %collective-permute-done = f32[]{:T(128)} collective-permute-done((f32[]{:T(128)}, f32[]{:T(128)}, u32[]{:S(2)}, u32[]{:S(2)}) %collective-permute-start) | collective-permute-done | bytes 36 | tf_op jit(solution)/shard_map/while/body/eval_jaxpr/ppermute | solution.py:14
  138.3 1.3 collective-permute-start.1
  139.6 1.3 collective-permute-start
  140.9 7.9 %collective-permute-done = f32[]{:T(128)} collective-permute-done((f32[]{:T(128)}, f32[]{:T(128)}, u32[]{:S(2)}, u32[]{:S(2)}) %collective-permute-start) | collective-permute-done | bytes 36 | tf_op jit(solution)/shard_map/while/body/eval_jaxpr/ppermute | solution.py:14
  149.7 1.3 collective-permute-start.1
  151.0 1.3 collective-permute-start
  152.3 7.9 %collective-permute-done = f32[]{:T(128)} collective-permute-done((f32[]{:T(128)}, f32[]{:T(128)}, u32[]{:S(2)}, u32[]{:S(2)}) %collective-permute-start) | collective-permute-done | bytes 36 | tf_op jit(solution)/shard_map/while/body/eval_jaxpr/ppermute | solution.py:14
  161.0 12.4 %while.37 = (s32[]{:T(128)}, f32[16,64,128]{2,1,0:T(8,128)S(1)}, f32[6,16,64,128]{3,2,1,0:T(8,128)}, f32[6,16]{1,0:T(8,128)S(1)}, f32[6,16,64,128]{3,2,1,0:T(8,128)}, /*index=5*/s32[]{:T(128)}) while((s32[]{:T(128)}, f32[16,64,128]{2,1,0:T(8,128)S(1)}, f32[6,16,64,128]{3,2,1,0:T(8,128)}, f32[6,16]{1,0:T(8,128)S(1)}, ...), condition=%wide.region_8.9_spmd, body=%wide.region_7.8_spmd.sunk | while | flops 262146 | bytes 2622221 | solution.py:42
  173.4 3.0 %fusion.22 = f32[6,16,64,256]{3,2,1,0:T(8,128)S(1)} fusion(bf16[6,256,128,1]{2,1,3,0:T(8,128)(2,1)S(1)} %bitcast.81, f32[6,16,64,128]{3,2,1,0:T(8,128)} %get-tuple-element.128), kind=kOutput, calls=%fused_computation.39 | convolution fusion | flops 403439616 | bytes 9830400 | tf_op jit(solution)/shard_map/ktn,khpn->kthp/dot_general | solution.py:49
  176.6 8.8 %fusion.1 = f32[6,16,256,64]{2,3,1,0:T(8,128)} fusion(f32[6,256,16]{1,2,0:T(8,128)S(1)} %copy-done.9, f32[6,256,16]{1,2,0:T(8,128)S(1)} %copy-done.8, f32[6,256,256]{2,1,0:T(8,128)S(1)} %fusion.30, pred[6,256,256]{2,1,0:T(8,128)(4,1)S(1)} %copy-done.6, bf16[6,256,16,64]{1,0,3,2:T(8,128)(2,1)S(1)} %copy-done.1), kind=kOutput, calls=%fused_computation.10 | convolution fusion | flops 836763648 | bytes 11599872 | tf_op jit(solution)/shard_map/ktsh,kshp->kthp/dot_general | solution.py:80
  185.4 4.2 %fusion.10 = bf16[6,256,16,64]{1,3,2,0:T(8,128)(2,1)S(1)} fusion(f32[6,16,256,64]{2,3,1,0:T(8,128)} %fusion.1, f32[6,16,64,256]{3,2,1,0:T(8,128)S(1)} %fusion.22, f32[16]{0:T(128)S(1)} %copy-done.12, f32[6,256,16]{1,2,0:T(8,128)S(1)} %copy-done.5, bf16[6,256,128,1]{2,1,3,0:T(8,128)(2,1)S(1)} %bitcast.82, f32[6,16,64,128]{3,2,1,0:T(8,128)S(1)} %copy-done.2, ...), kind=kOutput, calls=%fused_computation.23 | convolution fusion | flops 416808960 | bytes 22511680 | tf_op jit(solution)/shard_map/ktn,khpn->kthp/dot_general | solution.py:50
  189.6 4.3 %copy.90 = bf16[6,256,16,64]{1,0,3,2:T(8,128)(2,1)} copy(bf16[6,256,16,64]{1,3,2,0:T(8,128)(2,1)S(1)} %fusion.10) | data formatting | bytes 6291456 | tf_op jit(solution)/shard_map/convert_element_type | solution.py:114
  193.9 6.4 %all_to_all.37 = bf16[4,384,1024]{1,0,2:T(4,128)(2,1)S(1)} reshape(bf16[6,256,16,64]{1,0,3,2:T(8,128)(2,1)} %copy.90) | data formatting | bytes 6291456 | tf_op jit(solution)/shard_map/all_to_all | solution.py:115
  200.4 2.0 copy.91
  202.4 4.0 %all-to-all-start.2 = ((bf16[4,384,1024]{1,2,0:T(8,128)(2,1)}), bf16[4,384,1024]{1,2,0:T(8,128)(2,1)S(1)}, u32[]{:S(2)}, u32[]{:S(2)}) async-start(bf16[4,384,1024]{1,2,0:T(8,128)(2,1)} %copy.91), calls=%async_computation.2 | async-start | bytes 6291456 | tf_op jit(solution)/shard_map/all_to_all | solution.py:115
  206.4 4.6 %copy.92 = bf16[384,4096]{0,1:T(8,128)(2,1)} copy(bf16[384,4096]{1,0:T(8,128)(2,1)} %param.16) | data formatting | bytes 6291456 | tf_op args[1]
  211.1 65.5 %all-to-all-done.2 = bf16[4,384,1024]{1,2,0:T(8,128)(2,1)S(1)} async-done(((bf16[4,384,1024]{1,2,0:T(8,128)(2,1)}), bf16[4,384,1024]{1,2,0:T(8,128)(2,1)S(1)}, u32[]{:S(2)}, u32[]{:S(2)}) %all-to-all-start.2) | async-done | bytes 3145760 | tf_op jit(solution)/shard_map/all_to_all | solution.py:115
  276.6 3.7 %multiply_reduce_fusion = f32[384]{0:T(512)S(1)} fusion(bf16[384,4096]{0,1:T(8,128)(2,1)} %copy.92, bf16[4,384,1024]{1,2,0:T(8,128)(2,1)S(1)} %all-to-all-done.2), kind=kLoop, calls=%fused_computation.31 | loop fusion | flops 14155392 | bytes 6292992 | tf_op jit(solution)/shard_map/reduce_sum | solution.py:117
  280.4 3.6 %multiply_convert_fusion.2 = bf16[384,4096]{0,1:T(8,128)(2,1)} fusion(f32[4096]{0:T(1024)S(1)} %copy-done.10, f32[384]{0:T(512)S(1)} %add_rsqrt_fusion, bf16[384,4096]{0,1:T(8,128)(2,1)S(1)} %copy-done, bf16[4,384,1024]{1,2,0:T(8,128)(2,1)S(1)} %all-to-all-done.2), kind=kLoop, calls=%fused_computation.30 | loop fusion | flops 15728640 | bytes 9455104 | tf_op jit(solution)/shard_map/convert_element_type | solution.py:118
  283.9 4.6 %copy.93 = bf16[384,4096]{1,0:T(8,128)(2,1)} copy(bf16[384,4096]{0,1:T(8,128)(2,1)} %multiply_convert_fusion.2) | data formatting | bytes 6291456 | tf_op jit(solution)/shard_map/convert_element_type | solution.py:118
  (109 shorter events, 28.3 us)
Async XLA Ops:
  0.0 9.2 %all-to-all-start = ((bf16[384,4,16]{0,2,1:T(8,128)(2,1)}), bf16[384,4,16]{0,2,1:T(8,128)(2,1)S(1)}, u32[]{:S(2)}, u32[]{:S(2)}) async-start(bf16[384,4,16]{0,2,1:T(8,128)(2,1)} %bitcast.87), calls=%async_computation | async-start | bytes 98304 | tf_op jit(solution)/shard_map/all_to_all | solution.py:57
  9.2 4.8 %copy-start.11 = (s32[1536]{0:T(1024)S(1)}, s32[1536]{0:T(1024)}, u32[]{:S(2)}) copy-start(s32[1536]{0:T(1024)} %param.19) | copy-start | bytes 18436
  9.2 4.9 %copy-start.14 = (f32[16]{0:T(128)S(1)}, f32[16]{0:T(128)}, u32[]{:S(2)}) copy-start(f32[16]{0:T(128)} %param.21) | copy-start | bytes 196
  9.2 9.9 %copy-start.7 = (bf16[384,256]{1,0:T(8,128)(2,1)S(1)}, bf16[384,256]{1,0:T(8,128)(2,1)}, u32[]{:S(2)}) copy-start(bf16[384,256]{1,0:T(8,128)(2,1)} %param.17) | copy-start | bytes 589828
  9.2 94.3 %all-to-all-start.1 = ((bf16[384,4,1024]{0,2,1:T(8,128)(2,1)}), bf16[384,4,1024]{0,2,1:T(8,128)(2,1)}, u32[]{:S(2)}, u32[]{:S(2)}) async-start(bf16[384,4,1024]{0,2,1:T(8,128)(2,1)} %bitcast.9), calls=%async_computation.1 | async-start | bytes 6291456 | tf_op jit(solution)/shard_map/all_to_all | solution.py:56
  14.0 82.7 %copy-start.13 = (f32[16]{0:T(128)S(1)}, f32[16]{0:T(128)}, u32[]{:S(2)}) copy-start(f32[16]{0:T(128)} %param.20) | copy-start | bytes 196
  95.4 0.8 copy-start.3
  109.5 7.5 %copy-start.4 = (bf16[1536,128]{1,0:T(8,128)(2,1)S(1)}, bf16[1536,128]{1,0:T(8,128)(2,1)}, u32[]{:S(2)}) copy-start(bf16[1536,128]{1,0:T(8,128)(2,1)} %copy-done.3) | copy-start | bytes 1179652
  129.2 8.3 %collective-permute-start.1 = (f32[16,64,128]{2,1,0:T(8,128)S(1)}, f32[16,64,128]{2,1,0:T(8,128)S(1)}, u32[]{:S(2)}, u32[]{:S(2)}) collective-permute-start(f32[16,64,128]{2,1,0:T(8,128)S(1)} %multiply_add_fusion.2), channel_id=1, source_target_pairs={{0,4},{4,8},{8,12},{1,5},{5,9},{9,13},{2,6},{6,10},{10,14},{3,7},{... | collective-permute-start | bytes 1572872 | tf_op jit(solution)/shard_map/while/body/eval_jaxpr/ppermute | solution.py:14
  130.5 7.0 %collective-permute-start = (f32[]{:T(128)}, f32[]{:T(128)}, u32[]{:S(2)}, u32[]{:S(2)}) collective-permute-start(f32[]{:T(128)} %select_n.53), channel_id=1, source_target_pairs={{0,4},{4,8},{8,12},{1,5},{5,9},{9,13},{2,6},{6,10},{10,14},{3,7},{... | collective-permute-start | bytes 20 | tf_op jit(solution)/shard_map/while/body/eval_jaxpr/ppermute | solution.py:14
  138.3 10.5 %collective-permute-start.1 = (f32[16,64,128]{2,1,0:T(8,128)S(1)}, f32[16,64,128]{2,1,0:T(8,128)S(1)}, u32[]{:S(2)}, u32[]{:S(2)}) collective-permute-start(f32[16,64,128]{2,1,0:T(8,128)S(1)} %multiply_add_fusion.2), channel_id=1, source_target_pairs={{0,4},{4,8},{8,12},{1,5},{5,9},{9,13},{2,6},{6,10},{10,14},{3,7},{... | collective-permute-start | bytes 1572872 | tf_op jit(solution)/shard_map/while/body/eval_jaxpr/ppermute | solution.py:14
  139.6 9.2 %collective-permute-start = (f32[]{:T(128)}, f32[]{:T(128)}, u32[]{:S(2)}, u32[]{:S(2)}) collective-permute-start(f32[]{:T(128)} %select_n.53), channel_id=1, source_target_pairs={{0,4},{4,8},{8,12},{1,5},{5,9},{9,13},{2,6},{6,10},{10,14},{3,7},{... | collective-permute-start | bytes 20 | tf_op jit(solution)/shard_map/while/body/eval_jaxpr/ppermute | solution.py:14
  149.7 10.5 %collective-permute-start.1 = (f32[16,64,128]{2,1,0:T(8,128)S(1)}, f32[16,64,128]{2,1,0:T(8,128)S(1)}, u32[]{:S(2)}, u32[]{:S(2)}) collective-permute-start(f32[16,64,128]{2,1,0:T(8,128)S(1)} %multiply_add_fusion.2), channel_id=1, source_target_pairs={{0,4},{4,8},{8,12},{1,5},{5,9},{9,13},{2,6},{6,10},{10,14},{3,7},{... | collective-permute-start | bytes 1572872 | tf_op jit(solution)/shard_map/while/body/eval_jaxpr/ppermute | solution.py:14
  151.0 9.2 %collective-permute-start = (f32[]{:T(128)}, f32[]{:T(128)}, u32[]{:S(2)}, u32[]{:S(2)}) collective-permute-start(f32[]{:T(128)} %select_n.53), channel_id=1, source_target_pairs={{0,4},{4,8},{8,12},{1,5},{5,9},{9,13},{2,6},{6,10},{10,14},{3,7},{... | collective-permute-start | bytes 20 | tf_op jit(solution)/shard_map/while/body/eval_jaxpr/ppermute | solution.py:14
  173.4 3.1 %copy-start.1 = (bf16[6,256,16,64]{1,0,3,2:T(8,128)(2,1)S(1)}, bf16[6,256,16,64]{1,0,3,2:T(8,128)(2,1)}, u32[]{:S(2)}) copy-start(bf16[6,256,16,64]{1,0,3,2:T(8,128)(2,1)} %reshape.157) | copy-start | bytes 9437188
  173.4 3.2 %copy-start.6 = (pred[6,256,256]{2,1,0:T(8,128)(4,1)S(1)}, pred[6,256,256]{2,1,0:T(8,128)(4,1)}, u32[]{:S(2)}) copy-start(pred[6,256,256]{2,1,0:T(8,128)(4,1)} %compare_and_fusion) | copy-start | bytes 1179652
  173.4 3.2 %copy-start.8 = (f32[6,256,16]{1,2,0:T(8,128)S(1)}, f32[6,256,16]{1,2,0:T(8,128)}, u32[]{:S(2)}) copy-start(f32[6,256,16]{1,2,0:T(8,128)} %copy.79) | copy-start | bytes 294916
  173.4 3.2 %copy-start.9 = (f32[6,256,16]{1,2,0:T(8,128)S(1)}, f32[6,256,16]{1,2,0:T(8,128)}, u32[]{:S(2)}) copy-start(f32[6,256,16]{1,2,0:T(8,128)} %copy.81) | copy-start | bytes 294916
  176.6 8.8 %copy-start.2 = (f32[6,16,64,128]{3,2,1,0:T(8,128)S(1)}, f32[6,16,64,128]{3,2,1,0:T(8,128)}, u32[]{:S(2)}) copy-start(f32[6,16,64,128]{3,2,1,0:T(8,128)} %get-tuple-element.128) | copy-start | bytes 9437188
  176.6 8.8 %copy-start.5 = (f32[6,256,16]{1,2,0:T(8,128)S(1)}, f32[6,256,16]{1,2,0:T(8,128)}, u32[]{:S(2)}) copy-start(f32[6,256,16]{1,2,0:T(8,128)} %copy.85) | copy-start | bytes 294916
  176.6 8.8 %copy-start.12 = (f32[16]{0:T(128)S(1)}, f32[16]{0:T(128)}, u32[]{:S(2)}) copy-start(f32[16]{0:T(128)} %param.22) | copy-start | bytes 196
  202.4 74.2 %all-to-all-start.2 = ((bf16[4,384,1024]{1,2,0:T(8,128)(2,1)}), bf16[4,384,1024]{1,2,0:T(8,128)(2,1)S(1)}, u32[]{:S(2)}, u32[]{:S(2)}) async-start(bf16[4,384,1024]{1,2,0:T(8,128)(2,1)} %copy.91), calls=%async_computation.2 | async-start | bytes 6291456 | tf_op jit(solution)/shard_map/all_to_all | solution.py:115
  211.1 69.3 %copy-start.10 = (f32[4096]{0:T(1024)S(1)}, f32[4096]{0:T(1024)}, u32[]{:S(2)}) copy-start(f32[4096]{0:T(1024)} %param.23) | copy-start | bytes 49156
  276.6 3.8 %copy-start = (bf16[384,4096]{0,1:T(8,128)(2,1)S(1)}, bf16[384,4096]{0,1:T(8,128)(2,1)}, u32[]{:S(2)}) copy-start(bf16[384,4096]{0,1:T(8,128)(2,1)} %copy.92) | copy-start | bytes 9437188
where the time goes:
time: 294 us; the launch traced here: 289 us
  waiting for transfers between devices  87 us (30%)
  blocking collectives  76.2 us (26%)
  local copies, waits for them, and re-layouts  50.4 us (17%)
  other arithmetic  28.3 us (10%)
  starting transfers between devices  21.2 us (7%)
  matrix products  21.2 us (7%)
    all_gather x1, blocking collectives, shards(): maps_all = lax.all_gather(bc, 'head', axis=0, tiled=True)  76.2 us
    all_to_all x1, waiting for transfers between devices, shards(): lax.all_to_all(ssm_out, 'head', split_axis=0, concat_axis=1, tiled=True)  65.5 us
    ppermute x6, waiting for transfers between devices, from_behind(): return lax.ppermute(array, axis, pairs)  21.5 us
    add x12, other arithmetic, advance(): return (mult_block[:, None, None] * carry + state_block, carry)  14 us
    unnamed x32, local copies, waits for them, and re-layouts  10.2 us
    dot_general x1, matrix products, shards(): jnp.einsum('ktsh,kshp->kthp', mixing, head_x, preferred_element_type=jnp....  8.79 us
    all_to_all x2, local copies, waits for them, and re-layouts, shards(): lax.all_to_all(ssm_out, 'head', split_axis=0, concat_axis=1, tiled=True)  8.48 us
    ppermute x6, starting transfers between devices, from_behind(): return lax.ppermute(array, axis, pairs)  7.76 us
  transfers between devices with their start and end apart: 9, of which 4 were waited for; matrix products, arithmetic and copies ran while one was open for 7% of the time, Pallas kernels for 0%

commit v1 on v0

v1 whole, which is shorter than its diff:
```python
import jax
import jax.numpy as jnp
from jax import lax
from jax.sharding import PartitionSpec as P

STATE = 128
EXTRA = 16
SPAN_AXES = ("ctx", "head")


def shards(xs, gate_in, bc, dt_raw, doc_ids, dt_bias, decay_rate, skip, norm_gain):
    f32, bf16 = jnp.float32, jnp.bfloat16
    tokens, columns = xs.shape
    heads = dt_raw.shape[1]
    hdim = columns // heads
    devices = lax.axis_size("ctx") * lax.axis_size("head")
    own = columns // devices
    params = lax.all_gather(
        jnp.stack([dt_bias, decay_rate, skip]), "head", axis=1, tiled=True
    )
    ids = lax.dynamic_slice(doc_ids, (lax.axis_index("head") * tokens,), (tokens,))
    dt = jax.nn.softplus(dt_raw.astype(f32) + params[0][None, :])
    lower = jnp.arange(tokens)[:, None] >= jnp.arange(tokens)[None, :]
    log_decay = -jnp.dot(
        lower.astype(f32), dt * params[1][None, :], precision=lax.Precision.HIGHEST
    )
    log_end = log_decay[-1]
    middle = 0.5 * log_end
    spread = lambda v: jnp.repeat(v, hdim, axis=-1)
    into = jnp.exp(middle[None, :] - log_decay) * dt
    out_of = jnp.exp(log_decay - middle[None, :])
    x = xs.astype(f32)
    weighted = (spread(into) * x).astype(bf16)
    in_b, in_c = bc[:, :STATE], bc[:, STATE:]
    scores = jnp.einsum("tn,sn->ts", in_c, in_b, preferred_element_type=f32)
    scores = jnp.where(lower & (ids[:, None] == ids[None, :]), scores, 0.0).astype(bf16)
    last_b = jnp.where((ids == ids[-1])[:, None], in_b, jnp.zeros_like(in_b))
    state = jnp.einsum("sn,sq->nq", last_b, weighted, preferred_element_type=f32)
    state = (state * spread(jnp.exp(middle))[None, :]).astype(bf16)
    factor = spread(jnp.exp(log_end))
    factor_hi = factor.astype(bf16)
    factor_lo = (factor - factor_hi.astype(f32)).astype(bf16)
    back = jnp.full((columns,), ids[-1].astype(bf16))
    extra = jnp.concatenate(
        [jnp.stack([factor_hi, factor_lo, back]), jnp.zeros((EXTRA - 3, columns), bf16)]
    )
    block = jnp.concatenate([state, extra])
    block = block.reshape(STATE + EXTRA, devices, own).transpose(1, 0, 2)
    got = lax.all_to_all(block, SPAN_AXES, split_axis=0, concat_axis=0, tiled=True)

    def advance(carry, piece):
        entering, before = carry
        mult = piece[STATE].astype(f32) + piece[STATE + 1].astype(f32)
        back_id = piece[STATE + 2].astype(f32)
        give = jnp.concatenate(
            [
                entering.astype(bf16),
                before[None].astype(bf16),
                jnp.zeros((EXTRA - 1, own), bf16),
            ]
        )
        keep = jnp.where(back_id == before, mult, 0.0)
        return (keep[None] * entering + piece[:STATE].astype(f32), back_id), give

    unused, give = lax.scan(
        advance, (jnp.zeros((STATE, own), f32), jnp.full((own,), -1.0, f32)), got
    )
    back_here = lax.all_to_all(give, SPAN_AXES, split_axis=0, concat_axis=0, tiled=True)
    back_here = back_here.transpose(1, 0, 2).reshape(STATE + EXTRA, columns)
    before = back_here[STATE, 0].astype(f32)
    inside_c = jnp.where((ids.astype(f32) == before)[:, None], in_c, jnp.zeros_like(in_c))
    carried = jnp.dot(inside_c, back_here[:STATE], preferred_element_type=f32)
    local = jnp.dot(scores, weighted, preferred_element_type=f32)
    ssm = (
        spread(out_of) * (local + carried * spread(jnp.exp(middle))[None, :])
        + spread(params[2])[None, :] * x
    )
    gated = ssm.astype(bf16).astype(f32) * jax.nn.silu(gate_in.astype(f32))
    scale = lax.rsqrt(jnp.mean(gated * gated, axis=-1, keepdims=True) + 1e-05)
    return (gated * scale * norm_gain[None, :]).astype(bf16)


def solution(mesh):
    rows = P(("groups", "ctx", "head"), None)
    return jax.shard_map(
        shards,
        mesh=mesh,
        in_specs=(rows, rows, rows, rows, P(("groups", "ctx")), P("head"), P("head"), P("head"), P()),
        out_specs=rows,
        check_vma=False,
    )
```

time: 294 us -> 153 us (0.52)
  blocking collectives: 76.2 us -> 9.49 us
  waiting for transfers between devices: 87 us -> 47.3 us
  local copies, waits for them, and re-layouts: 50.4 us -> 31.9 us
  starting transfers between devices: 21.2 us -> 12.6 us
  other arithmetic: 28.3 us -> 22.5 us
    all_gather x1, blocking collectives: 76.2 us -> 9.49 us  [shards(): lax.all_gather(jnp.stack([dt_bias, decay_rate, skip]), 'head', axis=1, ti...]
    ppermute x6 -> x0, waiting for transfers between devices: 21.5 us -> none  [from_behind(): return lax.ppermute(array, axis, pairs)]
    all_to_all x3 -> x2, waiting for transfers between devices: 65.5 us -> 47.3 us  [the longest x1 28.5 us: shards(): lax.all_to_all(block, SPAN_AXES, split_axis=0, concat_axis=0, tiled=True)]
    add x15 -> x32, other arithmetic: 14.4 us -> 0.93 us  [the longest x16 0.63 us: advance(): return ((keep[None] * entering + piece[:STATE].astype(f32), back_id), give)]
    all_to_all x3 -> x1, local copies, waits for them, and re-layouts: 14.5 us -> 1.62 us  [shards(): lax.all_to_all(give, SPAN_AXES, split_axis=0, concat_axis=0, tiled=True)]
    dynamic_update_slice x0 -> x16, other arithmetic: none -> 11.6 us  [shards(): lax.scan(advance, (jnp.zeros((STATE, own), f32), jnp.full((own,), -1.0, f...]
    unnamed x32 -> x7, local copies, waits for them, and re-layouts: 10.2 us -> 0.1 us
    convert_element_type x4 -> x16, local copies, waits for them, and re-layouts: 9 us -> 0.08 us  [advance(): before[None].astype(bf16)]
  transfers between devices with their start and end apart: 9 -> 2, of which waited for: 4 -> 2; matrix products, arithmetic and copies ran while one was open for 7% -> 7% of each run, Pallas kernels for 0% -> 0%
where the time goes in v1:
time: 153 us; the launch traced here: 150 us
  waiting for transfers between devices  47.3 us (31%)
  local copies, waits for them, and re-layouts  31.9 us (21%)
  matrix products  24 us (16%)
  other arithmetic  22.5 us (15%)
  starting transfers between devices  12.6 us (8%)
  blocking collectives  9.49 us (6%)
    all_to_all x1, waiting for transfers between devices, shards(): lax.all_to_all(block, SPAN_AXES, split_axis=0, concat_axis=0, tiled=True)  28.5 us
    all_to_all x1, waiting for transfers between devices, shards(): lax.all_to_all(give, SPAN_AXES, split_axis=0, concat_axis=0, tiled=True)  18.8 us
    dot_general x1, matrix products, shards(): local = jnp.dot(scores, weighted, preferred_element_type=f32)  14.2 us
    reshape x2, local copies, waits for them, and re-layouts, shards(): spread = lambda v: jnp.repeat(v, hdim, axis=-1)  13.4 us
    dynamic_update_slice x16, other arithmetic, shards(): lax.scan(advance, (jnp.zeros((STATE, own), f32), jnp.full((own,), -1.0, f...  11.6 us
    all_gather x1, blocking collectives, shards(): lax.all_gather(jnp.stack([dt_bias, decay_rate, skip]), 'head', axis=1, ti...  9.49 us
    all_to_all x1, starting transfers between devices, shards(): lax.all_to_all(block, SPAN_AXES, split_axis=0, concat_axis=0, tiled=True)  7.78 us
    broadcast_in_dim x6, local copies, waits for them, and re-layouts, shards(): spread = lambda v: jnp.repeat(v, hdim, axis=-1)  6.4 us
  transfers between devices with their start and end apart: 2, of which 2 were waited for; matrix products, arithmetic and copies ran while one was open for 7% of the time, Pallas kernels for 0%

profile of v1, /device:TPU:5, one launch (start us, length us, event | category | flops | bytes accessed | tf_op | source)
XLA Modules:
  0.0 150.2 jit_solution(1938761750910926963)
XLA Ops:
  0.0 0.8 dynamic_slice.7
  1.4 1.4 broadcast_compare_fusion
  4.1 9.5 %all-gather = f32[4,16,3]{1,2,0:T(4,128)S(1)} all-gather(f32[1,16,3]{1,2,0:T(4,128)S(1)} %maximum_bitcast_fusion.1), channel_id=1, replica_groups=mesh['groups'=2,'ctx'=4,'head'=4] {'head'}, dimensions={0}, use_global_device_ids=true | all-gather | bytes 960 | tf_op jit(solution)/shard_map/all_gather | solution.py:18
  13.7 1.3 convolution_negate_fusion
  15.2 0.9 exponential_multiply_fusion
  16.3 3.1 %broadcast_in_dim.69 = f32[384,64,64]{0,2,1:T(8,128)} broadcast(f32[384,64]{0,1:T(8,128)S(1)} %get-tuple-element.66), dimensions={0,1} | broadcast | bytes 6389760 | tf_op jit(solution)/shard_map/broadcast_in_dim | solution.py:29
  19.4 6.8 %copy.20 = f32[384,4096]{1,0:T(8,128)} copy(f32[384,4096]{0,1:T(8,128)} %bitcast.51) | data formatting | bytes 12582912 | tf_op jit(solution)/shard_map/reshape | solution.py:29
  26.2 3.7 %fusion.12 = bf16[128,4096]{1,0:T(8,128)(2,1)S(1)} fusion(f32[4096]{0:T(1024)S(1)} %mul.100, pred[384]{0:T(512)(128)(4,1)S(1)} %broadcast_compare_fusion, bf16[384,256]{1,0:T(8,128)(2,1)S(1)} %copy-done.1, f32[384,4096]{1,0:T(8,128)} %copy.20, bf16[384,4096]{1,0:T(8,128)(2,1)S(1)} %copy-done), kind=kOutput, calls=%fused_computation.27 | convolution fusion | flops 408469504 | bytes 10600960 | tf_op jit(solution)/shard_map/sn,sq->nq/dot_general | solution.py:38
  30.3 5.4 %concatenate.10 = bf16[144,16,256]{2,0,1:T(8,128)(2,1)} concatenate(bf16[128,16,256]{2,0,1:T(8,128)(2,1)S(1)} %bitcast.55, bf16[1,16,256]{2,0,1:T(2,128)(2,1)S(1)} %get-tuple-element.69, bf16[1,16,256]{2,0,1:T(2,128)(2,1)S(1)} %get-tuple-element.68, bf16[1,16,256]{2,0,1:T(2,128)(2,1)S(1)} %stack_broadcast_in_dim.3, bf16[13,16,256]{2,0,1:T(8,128)(2,1)S(1)} %broadcast_in_dim.77), dimensions={0} | concatenate | bytes 2359296 | tf_op jit(solution)/shard_map/concatenate | solution.py:47
  35.7 7.8 %all-to-all-start = ((bf16[16,144,256]{2,1,0:T(8,128)(2,1)}), bf16[16,144,256]{2,1,0:T(8,128)(2,1)S(1)}, u32[]{:S(2)}, u32[]{:S(2)}) async-start(bf16[16,144,256]{2,1,0:T(8,128)(2,1)} %bitcast.11), calls=%async_computation | async-start | bytes 2359296 | tf_op jit(solution)/shard_map/all_to_all | solution.py:49
  43.5 28.5 %all-to-all-done = bf16[16,144,256]{2,1,0:T(8,128)(2,1)S(1)} async-done(((bf16[16,144,256]{2,1,0:T(8,128)(2,1)}), bf16[16,144,256]{2,1,0:T(8,128)(2,1)S(1)}, u32[]{:S(2)}, u32[]{:S(2)}) %all-to-all-start) | async-done | bytes 1179680 | tf_op jit(solution)/shard_map/all_to_all | solution.py:49
  72.1 15.2 %while.15 = (s32[]{:T(128)}, f32[128,256]{1,0:T(8,128)S(1)}, f32[256]{0:T(256)S(1)}, bf16[16,144,256]{2,1,0:T(8,128)(2,1)}, bf16[16,144,256]{2,1,0:T(8,128)(2,1)...) while((s32[]{:T(128)}, f32[128,256]{1,0:T(8,128)S(1)}, ...), condition=%wide.region_1.2_spmd.clone, body=%wide.region_0.1_spmd.clone.sunk | while | flops 386822 | bytes 677192 | solution.py:65
  75.2 0.7 fusion.57
  76.1 0.7 fusion.57
  77.1 0.7 fusion.57
  78.0 0.7 fusion.57
  79.0 0.7 fusion.57
  79.9 0.7 fusion.57
  80.9 0.7 fusion.57
  81.8 0.7 fusion.57
  82.8 0.7 fusion.57
  83.7 0.7 fusion.57
  87.3 4.9 %all-to-all-start.1 = ((bf16[16,144,256]{2,1,0:T(8,128)(2,1)}), bf16[16,144,256]{2,1,0:T(8,128)(2,1)S(1)}, u32[]{:S(2)}, u32[]{:S(2)}) async-start(bf16[16,144,256]{2,1,0:T(8,128)(2,1)} %get-tuple-element.32), calls=%async_computation.1 | async-start | bytes 2359296 | tf_op jit(solution)/shard_map/all_to_all | solution.py:68
  92.3 3.0 %broadcast_in_dim.67 = f32[384,64,64]{0,2,1:T(8,128)} broadcast(f32[384,64]{0,1:T(8,128)S(1)} %get-tuple-element.67), dimensions={0,1} | broadcast | bytes 6389760 | tf_op jit(solution)/shard_map/broadcast_in_dim | solution.py:29
  95.3 6.7 %copy.24 = f32[384,4096]{1,0:T(8,128)} copy(f32[384,4096]{0,1:T(8,128)} %bitcast.52) | data formatting | bytes 12582912 | tf_op jit(solution)/shard_map/reshape | solution.py:29
  102.0 18.8 %all-to-all-done.1 = bf16[16,144,256]{2,1,0:T(8,128)(2,1)S(1)} async-done(((bf16[16,144,256]{2,1,0:T(8,128)(2,1)}), bf16[16,144,256]{2,1,0:T(8,128)(2,1)S(1)}, u32[]{:S(2)}, u32[]{:S(2)}) %all-to-all-start.1) | async-done | bytes 1179680 | tf_op jit(solution)/shard_map/all_to_all | solution.py:68
  120.7 1.6 %copy.22 = bf16[16,144,256]{1,2,0:T(8,128)(2,1)S(1)} copy(bf16[16,144,256]{2,1,0:T(8,128)(2,1)S(1)} %all-to-all-done.1) | data formatting | bytes 2359296 | tf_op jit(solution)/shard_map/all_to_all | solution.py:68
  122.3 1.2 slice.63
  124.9 0.8 convert_compare_fusion
  125.7 4.8 %fusion.20 = f32[384,4096]{1,0:T(8,128)} fusion(bf16[128,4096]{0,1:T(8,128)(2,1)} %bitcast.56, pred[384]{0:T(512)(128)(4,1)S(1)} %convert_compare_fusion, bf16[384,256]{1,0:T(8,128)(2,1)S(1)} %copy-done.1), kind=kOutput, calls=%fused_computation.39 | convolution fusion | flops 402702336 | bytes 7438848 | tf_op jit(solution)/shard_map/dot_general | solution.py:72
  130.5 14.2 %multiply_reduce_fusion = (f32[384]{0:T(512)S(1)}, f32[384,4096]{1,0:T(8,128)}) fusion(bf16[384,4096]{1,0:T(8,128)(2,1)} %param.12, bf16[384,4096]{1,0:T(8,128)(2,1)} %param.11, f32[4096]{0:T(1024)S(1)} %mul.106, f32[384,4096]{1,0:T(8,128)} %copy.24, f32[384,4096]{1,0:T(8,128)} %fusion.20, f32[4096]{0:T(1024)S(1)} %mul.100, f32[384,4096]{1,0:T(8,128)} %copy.20, ...), kind=kOutput, calls=%fused_computation.25 | convolution fusion | flops 1276329600 | bytes 34838016 | tf_op jit(solution)/shard_map/dot_general | solution.py:73
  144.8 5.4 %multiply_convert_fusion = bf16[384,4096]{1,0:T(8,128)(2,1)} fusion(f32[384,4096]{1,0:T(8,128)} %get-tuple-element.74, f32[4096]{0:T(1024)S(1)} %copy-done.2, f32[384]{0:T(512)S(1)} %add_rsqrt_fusion), kind=kLoop, calls=%fused_computation.24 | loop fusion | flops 4718592 | bytes 9455104 | tf_op jit(solution)/shard_map/convert_element_type | solution.py:80
  (179 shorter events, 10.2 us)
Async XLA Ops:
  19.4 6.8 %copy-start = (bf16[384,4096]{1,0:T(8,128)(2,1)S(1)}, bf16[384,4096]{1,0:T(8,128)(2,1)}, u32[]{:S(2)}) copy-start(bf16[384,4096]{1,0:T(8,128)(2,1)} %param.11) | copy-start | bytes 9437188
  19.4 6.8 %copy-start.1 = (bf16[384,256]{1,0:T(8,128)(2,1)S(1)}, bf16[384,256]{1,0:T(8,128)(2,1)}, u32[]{:S(2)}) copy-start(bf16[384,256]{1,0:T(8,128)(2,1)} %param.13) | copy-start | bytes 589828
  35.7 36.3 %all-to-all-start = ((bf16[16,144,256]{2,1,0:T(8,128)(2,1)}), bf16[16,144,256]{2,1,0:T(8,128)(2,1)S(1)}, u32[]{:S(2)}, u32[]{:S(2)}) async-start(bf16[16,144,256]{2,1,0:T(8,128)(2,1)} %bitcast.11), calls=%async_computation | async-start | bytes 2359296 | tf_op jit(solution)/shard_map/all_to_all | solution.py:49
  87.3 33.4 %all-to-all-start.1 = ((bf16[16,144,256]{2,1,0:T(8,128)(2,1)}), bf16[16,144,256]{2,1,0:T(8,128)(2,1)S(1)}, u32[]{:S(2)}, u32[]{:S(2)}) async-start(bf16[16,144,256]{2,1,0:T(8,128)(2,1)} %get-tuple-element.32), calls=%async_computation.1 | async-start | bytes 2359296 | tf_op jit(solution)/shard_map/all_to_all | solution.py:68
  130.5 14.2 %copy-start.2 = (f32[4096]{0:T(1024)S(1)}, f32[4096]{0:T(1024)}, u32[]{:S(2)}) copy-start(f32[4096]{0:T(1024)} %param.19) | copy-start | bytes 49156

commit v2 on v1

v2 whole, which is shorter than its diff:
```python
import functools

import jax
import jax.numpy as jnp
from jax import lax
from jax.experimental import pallas as pl
from jax.experimental.pallas import tpu as pltpu
from jax.sharding import PartitionSpec as P

STATE = 128
EXTRA = 16
ROWS = STATE + EXTRA
MESH = pl.DeviceIdType.MESH
f32, bf16 = jnp.float32, jnp.bfloat16


def two_parts(v):
    hi = v.astype(bf16)
    return hi, (v - hi.astype(f32)).astype(bf16)


def dot(a, b):
    return jnp.dot(a, b, preferred_element_type=f32)


def kernel(
    n_ctx, n_head, owners,
    x_hbm, gate_hbm, bc, dt_raw, ids_col, ids_row, mine, gain,
    out_ref,
    x, gate, weighted, local, silu, square, into_s, out_s, decay_s, scores_s, last_b, rows_s, par,
    send1, recv1, send2, recv2,
    load_sem, par_ssem, par_rsem, ssem1, rsem1, ssem2, rsem2,
):
    tokens, columns = x.shape
    heads = dt_raw.shape[1]
    hdim = columns // heads
    own = columns // owners
    devices = n_ctx * n_head
    my_ctx, my_head = lax.axis_index("ctx"), lax.axis_index("head")
    me = my_ctx * n_head + my_head

    def place(d):
        return {"ctx": d // n_head, "head": lax.rem(d, n_head)}

    load_x = pltpu.make_async_copy(x_hbm, x, load_sem.at[0])
    load_gate = pltpu.make_async_copy(gate_hbm, gate, load_sem.at[1])
    load_x.start()
    load_gate.start()

    barrier = pltpu.get_barrier_semaphore()

    def greet(k, carry):
        peer = lax.rem(me + k, devices)
        pl.semaphore_signal(barrier, inc=1, device_id=place(peer), device_id_type=MESH)
        return carry

    lax.fori_loop(1, devices, greet, 0)
    pl.semaphore_wait(barrier, devices - 1)

    def par_copy(slot, peer, sem):
        return pltpu.make_async_remote_copy(
            src_ref=mine, dst_ref=par.at[slot],
            send_sem=par_ssem.at[sem], recv_sem=par_rsem.at[slot],
            device_id={"head": peer}, device_id_type=MESH,
        )

    for k in range(1, n_head):
        peer = lax.rem(my_head + k, n_head)
        par_copy(my_head, peer, peer).start()

    in_b, in_c = bc[:, :STATE], bc[:, STATE:]
    scores = lax.dot_general(in_c, in_b, (((1,), (1,)), ((), ())), preferred_element_type=f32)
    lower = lax.broadcasted_iota(jnp.int32, (tokens, tokens), 0) >= lax.broadcasted_iota(
        jnp.int32, (tokens, tokens), 1
    )
    same = ids_col[...] == ids_row[...]
    scores_s[...] = jnp.where(lower & same, scores, 0.0).astype(bf16)
    last_id = ids_row[:, tokens - 1 : tokens]
    last_b[...] = jnp.where(ids_col[...] == last_id, in_b.astype(f32), 0.0).astype(bf16)

    for k in range(1, n_head):
        peer = lax.rem(my_head + k, n_head)
        par_copy(peer, peer, peer).wait_recv()
    par[my_head] = mine[...]
    params = par[0]
    for k in range(1, n_head):
        params = params + par[k]
    bias, rate, skip = params[0:1, :heads], params[1:2, :heads], params[2:3, :heads]

    v = dt_raw[...].astype(f32) + bias
    dt = jnp.maximum(v, 0.0) + jnp.log1p(jnp.exp(-jnp.abs(v)))
    step = dt * rate
    step_hi, rest = two_parts(step)
    rest, step_lo = two_parts(step - step_hi.astype(f32))
    ones = lower.astype(f32).astype(bf16)
    log_decay = -(dot(ones, step_hi) + dot(ones, rest) + dot(ones, step_lo))
    log_end = log_decay[tokens - 1 : tokens, :]
    middle = 0.5 * log_end
    for ref, value in (
        (into_s, jnp.exp(middle - log_decay) * dt),
        (out_s, jnp.exp(log_decay - middle)),
        (decay_s, jnp.exp(log_decay)),
    ):
        ref[0], ref[1] = two_parts(value)
    at = lax.broadcasted_iota(jnp.int32, (EXTRA, heads), 0)
    end_row = jnp.exp(log_end)
    end_hi = end_row.astype(bf16).astype(f32)
    mid_row = jnp.exp(middle)
    mid_hi = mid_row.astype(bf16).astype(f32)
    skip_hi = skip.astype(bf16).astype(f32)
    pick = jnp.zeros((EXTRA, heads), f32)
    for i, row in enumerate(
        (end_hi, end_row - end_hi, last_id.astype(f32), mid_hi, mid_row - mid_hi, skip_hi, skip - skip_hi)
    ):
        pick = jnp.where(at == i, row, pick)
    rows_s[...] = pick.astype(bf16)
    load_x.wait()

    def selector(g):
        head = lax.broadcasted_iota(jnp.int32, (heads, own), 0)
        column = lax.broadcasted_iota(jnp.int32, (heads, own), 1) + g * own
        base = head * hdim
        return jnp.where((column >= base) & (column < base + hdim), 1.0, 0.0).astype(bf16)

    def spread(ref, sel):
        return dot(ref[0], sel) + dot(ref[1], sel)

    def part(g):
        return pl.ds(pl.multiple_of(g * own, own), own)

    def copy1(owner, slot, sem):
        return pltpu.make_async_remote_copy(
            src_ref=send1.at[owner], dst_ref=recv1.at[slot],
            send_sem=ssem1.at[owner], recv_sem=rsem1.at[sem],
            device_id=place(owner), device_id_type=MESH,
        )

    def copy2(peer, slot, sem):
        return pltpu.make_async_remote_copy(
            src_ref=send2.at[peer], dst_ref=recv2.at[slot],
            send_sem=ssem2.at[peer], recv_sem=rsem2.at[sem],
            device_id=place(peer), device_id_type=MESH,
        )

    def states(k, carry):
        g = lax.rem(me + k, owners)
        sel = selector(g)
        cols = part(g)
        w = (spread(into_s, sel) * x[:, cols].astype(f32)).astype(bf16)
        weighted[:, cols] = w
        extra = dot(rows_s[...], sel)
        mid = extra[3:4] + extra[4:5]
        state = lax.dot_general(
            last_b[...], w, (((0,), (0,)), ((), ())), preferred_element_type=f32
        )
        send1[g, 0:STATE, :] = (state * mid).astype(bf16)
        send1[g, STATE:ROWS, :] = extra.astype(bf16)

        @pl.when(g != me)
        def _():
            copy1(g, me, me).start()

        return carry

    lax.fori_loop(1, owners + 1, states, 0)
    load_gate.wait()

    def inside(g, carry):
        sel = selector(g)
        cols = part(g)
        extra = dot(rows_s[...], sel)
        skips = extra[5:6] + extra[6:7]
        y = dot(scores_s[...], weighted[:, cols])
        local[:, cols] = spread(out_s, sel) * y + skips * x[:, cols].astype(f32)
        v = gate[:, cols].astype(f32)
        silu[:, cols] = v / (1.0 + jnp.exp(-v))
        return carry

    lax.fori_loop(0, owners, inside, 0)

    def own_scan():
        recv1[me] = send1[me]

        def advance(j, carry):
            entering, before = carry

            @pl.when(j != me)
            def _():
                copy1(me, j, j).wait_recv()

            send2[j, 0:STATE, :] = entering.astype(bf16)
            send2[j, STATE:ROWS, :] = jnp.broadcast_to(before, (EXTRA, own)).astype(bf16)

            @pl.when(j != me)
            def _():
                copy2(j, me, me).start()

            tail = recv1[j, STATE:ROWS, :].astype(f32)
            back = tail[2:3]
            mult = jnp.where(back == before, tail[0:1] + tail[1:2], 0.0)
            entering = mult * entering + recv1[j, 0:STATE, :].astype(f32)
            return entering, back

        lax.fori_loop(
            0, devices, advance, (jnp.zeros((STATE, own), f32), jnp.full((1, own), -1.0, f32))
        )
        recv2[me] = send2[me]

    if owners == devices:
        own_scan()
    else:
        pl.when(me < owners)(own_scan)

    square[...] = jnp.zeros_like(square)

    def finish(k, carry):
        g = lax.rem(me + k, owners)

        @pl.when(g != me)
        def _():
            copy2(me, g, g).wait_recv()

        cols = part(g)
        before = recv2[g, STATE:ROWS, :].astype(f32)[0:1, 0:1]
        rows = jnp.where(ids_col[...].astype(f32) == before, in_c.astype(f32), 0.0).astype(bf16)
        carried = dot(rows, recv2[g, 0:STATE, :])
        ssm = local[:, cols] + spread(decay_s, selector(g)) * carried
        gated = ssm.astype(bf16).astype(f32) * silu[:, cols]
        local[:, cols] = gated
        total = square[...]
        for i in range(own // 128):
            piece = gated[:, i * 128 : (i + 1) * 128]
            total = total + piece * piece
        square[...] = total
        return carry

    lax.fori_loop(0, owners, finish, 0)
    mean = jnp.sum(square[...], axis=1, keepdims=True) * (1.0 / columns)
    scale = lax.rsqrt(mean + 1e-05)

    def store(g, carry):
        cols = part(g)
        out_ref[:, cols] = (local[:, cols] * scale * gain[:, cols]).astype(bf16)
        return carry

    lax.fori_loop(0, owners, store, 0)

    for k in range(1, n_head):
        peer = lax.rem(my_head + k, n_head)
        par_copy(my_head, peer, peer).wait_send()

    def drain1(g, carry):
        @pl.when(g != me)
        def _():
            copy1(g, me, me).wait_send()

        return carry

    lax.fori_loop(0, owners, drain1, 0)

    def drain2(j, carry):
        @pl.when(j != me)
        def _():
            copy2(j, me, me).wait_send()

        return carry

    def drain_all():
        lax.fori_loop(0, devices, drain2, 0)

    if owners == devices:
        drain_all()
    else:
        pl.when(me < owners)(drain_all)


def shards(xs, gate_in, bc, dt_raw, doc_ids, dt_bias, decay_rate, skip, norm_gain):
    tokens, columns = xs.shape
    heads = dt_raw.shape[1]
    n_ctx, n_head = lax.axis_size("ctx"), lax.axis_size("head")
    devices = n_ctx * n_head
    owners = min(devices, columns // 128)
    own = columns // owners
    at = lax.axis_index("head")
    ids = lax.dynamic_slice(doc_ids, (at * tokens,), (tokens,))
    stack = jnp.stack([dt_bias, decay_rate, skip])
    mine = jnp.where(
        (jnp.arange(heads) // (heads // n_head) == at)[None, :], jnp.tile(stack, (1, n_head)), 0.0
    )
    mine = jnp.pad(mine, ((0, 5), (0, 128 - heads)))
    vmem = pl.BlockSpec(memory_space=pltpu.VMEM)
    hbm = pl.BlockSpec(memory_space=pl.ANY)
    dma = pltpu.SemaphoreType.DMA
    return pl.pallas_call(
        functools.partial(kernel, n_ctx, n_head, owners),
        out_shape=jax.ShapeDtypeStruct((tokens, columns), bf16),
        in_specs=[hbm, hbm] + [vmem] * 6,
        out_specs=vmem,
        scratch_shapes=[
            pltpu.VMEM((tokens, columns), bf16),
            pltpu.VMEM((tokens, columns), bf16),
            pltpu.VMEM((tokens, columns), bf16),
            pltpu.VMEM((tokens, columns), f32),
            pltpu.VMEM((tokens, columns), f32),
            pltpu.VMEM((tokens, 128), f32),
            pltpu.VMEM((2, tokens, heads), bf16),
            pltpu.VMEM((2, tokens, heads), bf16),
            pltpu.VMEM((2, tokens, heads), bf16),
            pltpu.VMEM((tokens, tokens), bf16),
            pltpu.VMEM((tokens, STATE), bf16),
            pltpu.VMEM((EXTRA, heads), bf16),
            pltpu.VMEM((n_head, 8, 128), f32),
            pltpu.VMEM((owners, ROWS, own), bf16),
            pltpu.VMEM((devices, ROWS, own), bf16),
            pltpu.VMEM((devices, ROWS, own), bf16),
            pltpu.VMEM((owners, ROWS, own), bf16),
            dma((2,)), dma((n_head,)), dma((n_head,)),
            dma((owners,)), dma((devices,)), dma((devices,)), dma((owners,)),
        ],
        compiler_params=pltpu.CompilerParams(
            collective_id=0, has_side_effects=True, vmem_limit_bytes=52 * 2**20
        ),
        cost_estimate=pl.CostEstimate(
            flops=3 * 10**9, bytes_accessed=10**7, transcendentals=2 * 10**6
        ),
    )(
        xs, gate_in, bc, dt_raw, ids[:, None], ids[None, :], mine, norm_gain[None, :]
    )


def solution(mesh):
    rows = P(("groups", "ctx", "head"), None)
    return jax.shard_map(
        shards,
        mesh=mesh,
        in_specs=(rows, rows, rows, rows, P(("groups", "ctx")), P("head"), P("head"), P("head"), P()),
        out_specs=rows,
        check_vma=False,
    )
```

time: 153 us -> 84.2 us (0.55)
  the two profiles are of different devices: /device:TPU:5 before, /device:TPU:31 now
where the time goes in v2:
time: 84.2 us; the launch traced here: 83.8 us
  Pallas kernels  75.6 us (90%)
  local copies, waits for them, and re-layouts  7.44 us (9%)
    pallas_call x1, Pallas kernels, shards(): pl.pallas_call(functools.partial(kernel, n_ctx, n_head, owners), out_shap...  75.6 us
    unnamed x6, local copies, waits for them, and re-layouts  6.46 us

profile of v2, /device:TPU:31, one launch (start us, length us, event | category | flops | bytes accessed | tf_op | source)
XLA Modules:
  0.0 83.8 jit_solution(9323709730988183003)
XLA Ops:
  0.0 0.8 dynamic_slice.3
  0.8 0.7 pad_maximum_fusion
  1.5 0.1 tile.10
  1.6 0.9 %copy.11.dt_raw = bf16[384,64]{1,0:T(8,128)(2,1)S(1)} copy(bf16[384,64]{0,1:T(8,128)(2,1)} %param.12) | data formatting | bytes 98304 | tf_op args[3]
  2.5 0.1 broadcast_in_dim.27.ids_col
  2.6 0.0 copy-start
  2.6 0.9 %copy-done = bf16[384,256]{1,0:T(8,128)(2,1)S(1)} copy-done((bf16[384,256]{1,0:T(8,128)(2,1)S(1)}, bf16[384,256]{1,0:T(8,128)(2,1)}, u32[]{:S(2)}) %copy-start) | copy-done | bytes 196632
  3.5 0.0 copy-start.1
  3.5 0.7 copy-done.1
  4.3 75.6 %shard_map.91 = bf16[384,4096]{1,0:T(8,128)(2,1)} custom-call(bf16[384,4096]{1,0:T(8,128)(2,1)} %x_hbm.1, bf16[384,4096]{1,0:T(8,128)(2,1)} %gate_hbm.1, bf16[384,256]{1,0:T(8,128)(2,1)S(1)} %copy-done, bf16[384,64]{1,0:T(8,128)(2,1)S(1)} %copy.11.dt_raw, s32[384,1]{1,0:T(8,128)S(1)} %broadcast_in_dim.27.ids_col, s32[1,384]{1,0:T(1,128)S(1)} %broadcast_in_dim.23.ids_row, ...), custom_call_target="tpu_custom_call" | custom-call | flops 3000000000 | bytes 10000000 | tf_op jit(solution)/shard_map/pallas_call | solution.py:294
  79.9 3.9 %copy.14 = bf16[384,4096]{1,0:T(8,128)(2,1)} copy(bf16[384,4096]{1,0:T(8,128)(2,1)} %shard_map.91) | data formatting | bytes 6291456
  (5 shorter events, 0.0 us)
Async XLA Ops:
  2.6 0.9 %copy-start = (bf16[384,256]{1,0:T(8,128)(2,1)S(1)}, bf16[384,256]{1,0:T(8,128)(2,1)}, u32[]{:S(2)}) copy-start(bf16[384,256]{1,0:T(8,128)(2,1)} %bc.1) | copy-start | bytes 589828
  3.5 0.7 copy-start.1

commit v3 on v2

v3 whole, which is shorter than its diff:
```python
import functools

import jax
import jax.numpy as jnp
from jax import lax
from jax.experimental import pallas as pl
from jax.experimental.pallas import tpu as pltpu
from jax.sharding import PartitionSpec as P

STATE = 128
EXTRA = 16
WIDTH = 256
LAG = 2
MESH = pl.DeviceIdType.MESH
f32, bf16 = jnp.float32, jnp.bfloat16


def two_parts(v):
    hi = v.astype(bf16)
    return hi, (v - hi.astype(f32)).astype(bf16)


def dot(a, b):
    return jnp.dot(a, b, preferred_element_type=f32)


def kernel(
    n_ctx, n_head, chunks, lag,
    x_hbm, gate_hbm, bc, dt_raw, ids_col, ids_row, mine, backs,
    gated_ref, scale_ref,
    x, gate, into_s, out_s, decay_s, scores_s, last_b, in_c_s, rows_s, par, end_tile, ends, prev,
    state_s, send_r, send_u, send_v, recv_r, recv_u, recv_v, square,
    load_sem, par_ssem, par_rsem, end_ssem, end_rsem, prev_sem, r_ssem, r_rsem, u_ssem, u_rsem, v_ssem, v_rsem,
    weighted,
):
    tokens, columns = x.shape
    heads = dt_raw.shape[1]
    hdim = columns // heads
    own = columns // chunks
    my_ctx, my_head = lax.axis_index("ctx"), lax.axis_index("head")
    has_prev, has_next = my_ctx > 0, my_ctx < n_ctx - 1
    has_low, has_high = my_head > 0, my_head < n_head - 1
    next_ctx = jnp.minimum(my_ctx + 1, n_ctx - 1)
    high = jnp.minimum(my_head + 1, n_head - 1)
    low = jnp.maximum(my_head - 1, 0)

    load_x = pltpu.make_async_copy(x_hbm, x, load_sem.at[0])
    load_gate = pltpu.make_async_copy(gate_hbm, gate, load_sem.at[1])
    load_x.start()
    load_gate.start()

    barrier = pltpu.get_barrier_semaphore()
    for k in range(1, n_head):
        peer = lax.rem(my_head + k, n_head)
        pl.semaphore_signal(barrier, inc=1, device_id={"head": peer}, device_id_type=MESH)

    @pl.when(has_prev)
    def _():
        pl.semaphore_signal(barrier, inc=1, device_id={"ctx": my_ctx - 1}, device_id_type=MESH)

    @pl.when(has_next)
    def _():
        pl.semaphore_signal(barrier, inc=1, device_id={"ctx": my_ctx + 1}, device_id_type=MESH)

    neighbours = jnp.minimum(my_ctx, 1) + jnp.minimum(n_ctx - 1 - my_ctx, 1)
    pl.semaphore_wait(barrier, n_head - 1 + neighbours)

    def tile_copy(src, dst, ssem, rsem, slot, peer, sem):
        return pltpu.make_async_remote_copy(
            src_ref=src, dst_ref=dst.at[slot], send_sem=ssem.at[sem], recv_sem=rsem.at[slot],
            device_id={"head": peer}, device_id_type=MESH,
        )

    prev_copy = pltpu.make_async_remote_copy(
        src_ref=backs, dst_ref=prev, send_sem=prev_sem.at[0], recv_sem=prev_sem.at[1],
        device_id={"ctx": next_ctx}, device_id_type=MESH,
    )
    peers = [lax.rem(my_head + k, n_head) for k in range(1, n_head)]
    for peer in peers:
        tile_copy(mine, par, par_ssem, par_rsem, my_head, peer, peer).start()
    pl.when(has_next)(prev_copy.start)

    in_b, in_c = bc[:, :STATE], bc[:, STATE:]
    scores = lax.dot_general(in_c, in_b, (((1,), (1,)), ((), ())), preferred_element_type=f32)
    lower = lax.broadcasted_iota(jnp.int32, (tokens, tokens), 0) >= lax.broadcasted_iota(
        jnp.int32, (tokens, tokens), 1
    )
    same = ids_col[...] == ids_row[...]
    scores_s[...] = jnp.where(lower & same, scores, 0.0).astype(bf16)
    last_id = ids_row[:, tokens - 1 : tokens]
    last_b[...] = jnp.where(ids_col[...] == last_id, in_b.astype(f32), 0.0).astype(bf16)

    for peer in peers:
        tile_copy(mine, par, par_ssem, par_rsem, peer, peer, peer).wait_recv()
    par[my_head] = mine[...]
    params = par[0]
    for k in range(1, n_head):
        params = params + par[k]
    bias, rate, skip = params[0:1, :heads], params[1:2, :heads], params[2:3, :heads]

    v = dt_raw[...].astype(f32) + bias
    dt = jnp.maximum(v, 0.0) + jnp.log1p(jnp.exp(-jnp.abs(v)))
    step = dt * rate
    step_hi = step.astype(bf16)
    rest, step_lo = two_parts(step - step_hi.astype(f32))
    ones = lower.astype(f32).astype(bf16)
    log_decay = -(dot(ones, step_hi) + dot(ones, rest) + dot(ones, step_lo))
    log_end = log_decay[tokens - 1 : tokens, :]
    end_tile[...] = jnp.zeros_like(end_tile)
    end_tile[0:1, :heads] = log_end
    for peer in peers:
        tile_copy(end_tile, ends, end_ssem, end_rsem, my_head, peer, peer).start()
    middle = 0.5 * log_end
    for ref, value in (
        (into_s, jnp.exp(middle - log_decay) * dt),
        (out_s, jnp.exp(log_decay - middle)),
        (decay_s, jnp.exp(log_decay)),
    ):
        ref[0], ref[1] = two_parts(value)

    @pl.when(my_ctx == 0)
    def _():
        prev[...] = jnp.full(prev.shape, -1.0, f32)
        recv_r[...] = jnp.zeros_like(recv_r)

    @pl.when(my_head == 0)
    def _():
        recv_u[...] = jnp.zeros_like(recv_u)

    @pl.when(my_head == n_head - 1)
    def _():
        recv_v[...] = jnp.zeros_like(recv_v)

    pl.when(has_prev)(prev_copy.wait_recv)
    for peer in peers:
        tile_copy(end_tile, ends, end_ssem, end_rsem, peer, peer, peer).wait_recv()
    ends[my_head] = end_tile[...]
    before = prev[n_head - 1 : n_head, :]
    my_before = before
    one = jnp.ones((1, heads), f32)
    ahead, through, after, whole, mine_m = one, one, one, one, one
    for z in range(n_head):
        back = backs[z : z + 1, :]
        my_before = jnp.where(my_head == z, before, my_before)
        m = jnp.where(back == before, jnp.exp(ends[z, 0:1, :]), 0.0)[:, :heads]
        before = back
        whole = whole * m
        ahead = jnp.where(z < my_head, ahead * m, ahead)
        through = jnp.where(z <= my_head, through * m, through)
        after = jnp.where(z > my_head, after * m, after)
        mine_m = jnp.where(my_head == z, m, mine_m)
    in_c_s[...] = jnp.where(
        ids_col[...].astype(f32) == my_before[:, 0:1], in_c.astype(f32), 0.0
    ).astype(bf16)
    at = lax.broadcasted_iota(jnp.int32, (EXTRA, heads), 0)
    pick = jnp.zeros((EXTRA, heads), f32)
    for i, row in enumerate((jnp.exp(middle), skip, mine_m, ahead, through, after, whole)):
        top = row.astype(bf16).astype(f32)
        pick = jnp.where(at == 2 * i, top, pick)
        pick = jnp.where(at == 2 * i + 1, row - top, pick)
    rows_s[...] = pick.astype(bf16)
    square[...] = jnp.zeros_like(square)
    load_x.wait()
    load_gate.wait()

    def selector(g):
        head = lax.broadcasted_iota(jnp.int32, (heads, own), 0)
        column = lax.broadcasted_iota(jnp.int32, (heads, own), 1) + g * own
        base = head * hdim
        return jnp.where((column >= base) & (column < base + hdim), 1.0, 0.0).astype(bf16)

    def spread(ref, sel):
        return dot(ref[0], sel) + dot(ref[1], sel)

    def part(g):
        return pl.ds(pl.multiple_of(g * own, own), own)

    def spread_rows(sel):
        extra = dot(rows_s[...], sel)
        return [extra[2 * i : 2 * i + 1] + extra[2 * i + 1 : 2 * i + 2] for i in range(7)]

    def chain(src, dst, ssem, rsem, g, to):
        return pltpu.make_async_remote_copy(
            src_ref=src.at[g], dst_ref=dst.at[g], send_sem=ssem.at[g], recv_sem=rsem.at[g],
            device_id=to, device_id_type=MESH,
        )

    def copy_r(g):
        return chain(send_r, recv_r, r_ssem, r_rsem, g, {"ctx": next_ctx})

    def copy_u(g):
        return chain(send_u, recv_u, u_ssem, u_rsem, g, {"head": high})

    def copy_v(g):
        return chain(send_v, recv_v, v_ssem, v_rsem, g, {"head": low})

    def first(g):
        sel = selector(g)
        mid, _, _, _, _, after_g, whole_g = spread_rows(sel)
        w = (spread(into_s, sel) * x[:, part(g)].astype(f32)).astype(bf16)
        weighted[:, part(g)] = w
        state = mid * lax.dot_general(
            last_b[...], w, (((0,), (0,)), ((), ())), preferred_element_type=f32
        )
        state_s[g] = state

        @pl.when(has_prev)
        def _():
            copy_r(g).wait_recv()

        @pl.when(has_next)
        def _():
            send_r[g] = (whole_g * recv_r[g].astype(f32) + after_g * state).astype(bf16)
            copy_r(g).start()

    def upward(g):
        @pl.when(has_low)
        def _():
            copy_u(g).wait_recv()

        @pl.when(has_high)
        def _():
            _, _, m, _, through_g, _, _ = spread_rows(selector(g))
            send_u[g] = (
                m * recv_u[g].astype(f32) + state_s[g] + through_g * recv_r[g].astype(f32)
            ).astype(bf16)
            copy_u(g).start()

    def downward(g):
        @pl.when(has_high)
        def _():
            copy_v(g).wait_recv()

        @pl.when(has_low)
        def _():
            send_v[g] = (recv_v[g].astype(f32) + recv_r[g].astype(f32)).astype(bf16)
            copy_v(g).start()

    def finish(g):
        sel = selector(g)
        cols = part(g)
        mid, skips, _, ahead_g, _, _, _ = spread_rows(sel)
        entering = recv_u[g].astype(f32) + ahead_g * (
            recv_v[g].astype(f32) + recv_r[g].astype(f32)
        )
        y = dot(scores_s[...], weighted[:, cols])
        carried = dot(in_c_s[...], entering.astype(bf16))
        ssm = (
            spread(out_s, sel) * y
            + spread(decay_s, sel) * carried
            + skips * x[:, cols].astype(f32)
        )
        v = gate[:, cols].astype(f32)
        gated = ssm.astype(bf16).astype(f32) * (v / (1.0 + jnp.exp(-v)))
        gated_ref[:, cols] = gated.astype(bf16)
        total = square[...]
        for i in range(own // 128):
            piece = gated[:, i * 128 : (i + 1) * 128]
            total = total + piece * piece
        square[...] = total

    up_lag = lag * my_head
    down_lag = lag * (n_head - 1 - my_head)
    end_lag = lag * (n_head - 1)

    def turn(i, carry):
        for stage, behind in ((first, 0), (upward, up_lag), (downward, down_lag), (finish, end_lag)):
            g = i - behind

            @pl.when((g >= 0) & (g < chunks))
            def _(stage=stage, g=g):
                stage(g)

        return carry

    lax.fori_loop(0, chunks + end_lag, turn, 0)
    mean = jnp.sum(square[...], axis=1, keepdims=True) * (1.0 / columns)
    scale_ref[...] = jnp.broadcast_to(lax.rsqrt(mean + 1e-05), scale_ref.shape)

    for peer in peers:
        tile_copy(mine, par, par_ssem, par_rsem, my_head, peer, peer).wait_send()
        tile_copy(end_tile, ends, end_ssem, end_rsem, my_head, peer, peer).wait_send()
    pl.when(has_next)(prev_copy.wait_send)

    def drain(g, carry):
        pl.when(has_next)(copy_r(g).wait_send)
        pl.when(has_high)(copy_u(g).wait_send)
        pl.when(has_low)(copy_v(g).wait_send)
        return carry

    lax.fori_loop(0, chunks, drain, 0)


def shards(xs, gate_in, bc, dt_raw, doc_ids, dt_bias, decay_rate, skip, norm_gain):
    tokens, columns = xs.shape
    heads = dt_raw.shape[1]
    n_ctx, n_head = lax.axis_size("ctx"), lax.axis_size("head")
    chunks = columns // WIDTH
    at = lax.axis_index("head")
    ids = lax.dynamic_slice(doc_ids, (at * tokens,), (tokens,))
    stack = jnp.stack([dt_bias, decay_rate, skip])
    mine = jnp.where(
        (jnp.arange(heads) // (heads // n_head) == at)[None, :], jnp.tile(stack, (1, n_head)), 0.0
    )
    mine = jnp.pad(mine, ((0, 5), (0, 128 - heads)))
    tall = max(8, n_head)
    backs = doc_ids.reshape(n_head, tokens)[:, -1].astype(f32)
    backs = jnp.broadcast_to(jnp.pad(backs, (0, tall - n_head))[:, None], (tall, 128))
    vmem = pl.BlockSpec(memory_space=pltpu.VMEM)
    hbm = pl.BlockSpec(memory_space=pl.ANY)
    dma = pltpu.SemaphoreType.DMA
    travel = pltpu.VMEM((chunks, STATE, WIDTH), bf16)
    pair = pltpu.VMEM((2, tokens, heads), bf16)
    gated, scale = pl.pallas_call(
        functools.partial(kernel, n_ctx, n_head, chunks, LAG),
        out_shape=(
            jax.ShapeDtypeStruct((tokens, columns), bf16),
            jax.ShapeDtypeStruct((tokens, 128), f32),
        ),
        in_specs=[hbm, hbm] + [vmem] * 6,
        out_specs=(vmem, vmem),
        scratch_shapes=[
            pltpu.VMEM((tokens, columns), bf16),
            pltpu.VMEM((tokens, columns), bf16),
            pair, pair, pair,
            pltpu.VMEM((tokens, tokens), bf16),
            pltpu.VMEM((tokens, STATE), bf16),
            pltpu.VMEM((tokens, STATE), bf16),
            pltpu.VMEM((EXTRA, heads), bf16),
            pltpu.VMEM((n_head, 8, 128), f32),
            pltpu.VMEM((8, 128), f32),
            pltpu.VMEM((n_head, 8, 128), f32),
            pltpu.VMEM((tall, 128), f32),
            pltpu.VMEM((chunks, STATE, WIDTH), f32),
            travel, travel, travel, travel, travel, travel,
            pltpu.VMEM((tokens, 128), f32),
            dma((2,)), dma((n_head,)), dma((n_head,)), dma((n_head,)), dma((n_head,)), dma((2,)),
        ]
        + [dma((chunks,))] * 6
        + [pltpu.VMEM((tokens, columns), bf16)],
        compiler_params=pltpu.CompilerParams(
            collective_id=0, has_side_effects=True, vmem_limit_bytes=44 * 2**20
        ),
        cost_estimate=pl.CostEstimate(
            flops=3 * 10**9, bytes_accessed=10**7, transcendentals=2 * 10**6
        ),
    )(xs, gate_in, bc, dt_raw, ids[:, None], ids[None, :], mine, backs)
    return (gated.astype(f32) * scale[:, :1] * norm_gain[None, :]).astype(bf16)


def solution(mesh):
    rows = P(("groups", "ctx", "head"), None)
    return jax.shard_map(
        shards,
        mesh=mesh,
        in_specs=(rows, rows, rows, rows, P(("groups", "ctx")), P("head"), P("head"), P("head"), P()),
        out_specs=rows,
        check_vma=False,
    )
```

time: 84.2 us -> 66.1 us (0.79)
  the two profiles are of different devices: /device:TPU:31 before, /device:TPU:5 now
where the time goes in v3:
time: 66.1 us; the launch traced here: 64.9 us
  Pallas kernels  53.7 us (81%)
  local copies, waits for them, and re-layouts  7.53 us (11%)
  other arithmetic  3.6 us (5%)
    pallas_call x1, Pallas kernels, shards(): pl.pallas_call(functools.partial(kernel, n_ctx, n_head, chunks, LAG), out...  53.7 us
    unnamed x9, local copies, waits for them, and re-layouts  5.62 us
    convert_element_type x1, other arithmetic, shards(): return (gated.astype(f32) * scale[:, :1] * norm_gain[None, :]).astype(bf16)  2.71 us

profile of v3, /device:TPU:5, one launch (start us, length us, event | category | flops | bytes accessed | tf_op | source)
XLA Modules:
  0.0 64.9 jit_solution(17167311244310662889)
XLA Ops:
  0.0 0.8 %dynamic_slice.3 = s32[384]{0:T(512)S(1)} dynamic-slice(s32[1536]{0:T(1024)} %param.13, s32[]{:T(128)S(6)} %select_n.16), dynamic_slice_sizes={384} | dynamic-slice | bytes 3076 | tf_op jit(solution)/shard_map/dynamic_slice | solution.py:300
  0.8 0.7 %pad_maximum_fusion = f32[3,16]{1,0:T(4,128)S(1)} fusion(f32[1,16]{1,0:T(1,128)} %bitcast.3, f32[1,16]{1,0:T(1,128)} %bitcast.4, f32[1,16]{1,0:T(1,128)} %bitcast.5), kind=kLoop, calls=%fused_computation.4 | loop fusion | flops 96 | bytes 384 | tf_op jit(solution)/shard_map/stack | solution.py:301
  1.5 0.1 tile.10
  1.6 0.7 %reshape.24 = s32[4,384]{1,0:T(4,128)S(1)} reshape(s32[1536]{0:T(1024)} %param.13) | data formatting | bytes 12288 | tf_op jit(solution)/shard_map/reshape | solution.py:307
  2.3 0.2 fusion
  2.5 0.1 broadcast_in_dim.30.backs
  2.6 0.9 %copy.13.dt_raw = bf16[384,64]{1,0:T(8,128)(2,1)S(1)} copy(bf16[384,64]{0,1:T(8,128)(2,1)} %param.12) | data formatting | bytes 98304 | tf_op args[3]
  3.5 0.1 broadcast_in_dim.31.ids_col
  3.6 0.0 copy-start
  3.6 1.9 %copy-done = bf16[384,4096]{1,0:T(8,128)(2,1)S(1)} copy-done((bf16[384,4096]{1,0:T(8,128)(2,1)S(1)}, bf16[384,4096]{1,0:T(8,128)(2,1)}, u32[]{:S(2)}) %copy-start) | copy-done | bytes 3145752
  5.5 0.0 copy-start.1
  5.5 1.9 %copy-done.1 = bf16[384,4096]{1,0:T(8,128)(2,1)S(1)} copy-done((bf16[384,4096]{1,0:T(8,128)(2,1)S(1)}, bf16[384,4096]{1,0:T(8,128)(2,1)}, u32[]{:S(2)}) %copy-start.1) | copy-done | bytes 3145752
  7.4 0.0 copy-start.2
  7.4 0.9 %copy-done.2 = bf16[384,256]{1,0:T(8,128)(2,1)S(1)} copy-done((bf16[384,256]{1,0:T(8,128)(2,1)S(1)}, bf16[384,256]{1,0:T(8,128)(2,1)}, u32[]{:S(2)}) %copy-start.2) | copy-done | bytes 196632
  8.3 0.0 copy-start.3
  8.3 53.7 %shard_map.91 = (bf16[384,4096]{1,0:T(8,128)(2,1)S(1)}, f32[384,128]{1,0:T(8,128)S(1)}) custom-call(bf16[384,4096]{1,0:T(8,128)(2,1)S(1)} %copy-done, bf16[384,4096]{1,0:T(8,128)(2,1)S(1)} %copy-done.1, bf16[384,256]{1,0:T(8,128)(2,1)S(1)} %copy-done.2, bf16[384,64]{1,0:T(8,128)(2,1)S(1)} %copy.13.dt_raw, s32[384,1]{1,0:T(8,128)S(1)} %broadcast_in_dim.31.ids_col, ...), custom_call_target="tpu_custom_call" | custom-call | flops 3000000000 | bytes 10000000 | tf_op jit(solution)/shard_map/pallas_call | solution.py:314
  62.1 0.1 slice_reduce_fusion
  62.2 0.0 copy-done.3
  62.2 2.7 %multiply_convert_fusion = bf16[384,4096]{1,0:T(8,128)(2,1)} fusion(bf16[384,4096]{1,0:T(8,128)(2,1)S(1)} %get-tuple-element.7, f32[4096]{0:T(1024)S(1)} %copy-done.3, f32[384]{0:T(512)S(1)} %slice_reduce_fusion), kind=kLoop, calls=%fused_computation | loop fusion | flops 6291456 | bytes 6309376 | tf_op jit(solution)/shard_map/convert_element_type | solution.py:348
  (6 shorter events, 0.0 us)
Async XLA Ops:
  3.6 1.9 %copy-start = (bf16[384,4096]{1,0:T(8,128)(2,1)S(1)}, bf16[384,4096]{1,0:T(8,128)(2,1)}, u32[]{:S(2)}) copy-start(bf16[384,4096]{1,0:T(8,128)(2,1)} %x_hbm.1) | copy-start | bytes 9437188
  5.5 1.9 %copy-start.1 = (bf16[384,4096]{1,0:T(8,128)(2,1)S(1)}, bf16[384,4096]{1,0:T(8,128)(2,1)}, u32[]{:S(2)}) copy-start(bf16[384,4096]{1,0:T(8,128)(2,1)} %gate_hbm.1) | copy-start | bytes 9437188
  7.4 0.9 %copy-start.2 = (bf16[384,256]{1,0:T(8,128)(2,1)S(1)}, bf16[384,256]{1,0:T(8,128)(2,1)}, u32[]{:S(2)}) copy-start(bf16[384,256]{1,0:T(8,128)(2,1)} %bc.1) | copy-start | bytes 589828
  8.3 53.9 %copy-start.3 = (f32[4096]{0:T(1024)S(1)}, f32[4096]{0:T(1024)}, u32[]{:S(2)}) copy-start(f32[4096]{0:T(1024)} %param.17) | copy-start | bytes 49156

commit v4 on v3

--- a/solution.py
+++ b/solution.py
@@ -10,7 +10,7 @@
 STATE = 128
 EXTRA = 16
 WIDTH = 256
-LAG = 2
+LAG = 3
 MESH = pl.DeviceIdType.MESH
 f32, bf16 = jnp.float32, jnp.bfloat16
 
@@ -31,7 +31,7 @@
     x, gate, into_s, out_s, decay_s, scores_s, last_b, in_c_s, rows_s, par, end_tile, ends, prev,
     state_s, send_r, send_u, send_v, recv_r, recv_u, recv_v, square,
     load_sem, par_ssem, par_rsem, end_ssem, end_rsem, prev_sem, r_ssem, r_rsem, u_ssem, u_rsem, v_ssem, v_rsem,
-    weighted,
+    weighted, sels,
 ):
     tokens, columns = x.shape
     heads = dt_raw.shape[1]
@@ -62,6 +62,14 @@
     def _():
         pl.semaphore_signal(barrier, inc=1, device_id={"ctx": my_ctx + 1}, device_id_type=MESH)
 
+    def make_selector(g, carry):
+        row = lax.broadcasted_iota(jnp.int32, (2 * heads, own), 0)
+        base = jnp.where(row >= heads, row - heads, row) * hdim
+        column = lax.broadcasted_iota(jnp.int32, (2 * heads, own), 1) + g * own
+        sels[g] = jnp.where((column >= base) & (column < base + hdim), 1.0, 0.0).astype(bf16)
+        return carry
+
+    lax.fori_loop(0, chunks, make_selector, 0)
     neighbours = jnp.minimum(my_ctx, 1) + jnp.minimum(n_ctx - 1 - my_ctx, 1)
     pl.semaphore_wait(barrier, n_head - 1 + neighbours)
 
@@ -88,7 +96,7 @@
     same = ids_col[...] == ids_row[...]
     scores_s[...] = jnp.where(lower & same, scores, 0.0).astype(bf16)
     last_id = ids_row[:, tokens - 1 : tokens]
-    last_b[...] = jnp.where(ids_col[...] == last_id, in_b.astype(f32), 0.0).astype(bf16)
+    last_b[...] = jnp.where(ids_col[...] == last_id, in_b.astype(f32), 0.0).T.astype(bf16)
 
     for peer in peers:
         tile_copy(mine, par, par_ssem, par_rsem, peer, peer, peer).wait_recv()
@@ -116,7 +124,7 @@
         (out_s, jnp.exp(log_decay - middle)),
         (decay_s, jnp.exp(log_decay)),
     ):
-        ref[0], ref[1] = two_parts(value)
+        ref[:, :heads], ref[:, heads:] = two_parts(value)
 
     @pl.when(my_ctx == 0)
     def _():
@@ -164,19 +172,16 @@
     load_gate.wait()
 
     def selector(g):
-        head = lax.broadcasted_iota(jnp.int32, (heads, own), 0)
-        column = lax.broadcasted_iota(jnp.int32, (heads, own), 1) + g * own
-        base = head * hdim
-        return jnp.where((column >= base) & (column < base + hdim), 1.0, 0.0).astype(bf16)
+        return sels[g]
 
     def spread(ref, sel):
-        return dot(ref[0], sel) + dot(ref[1], sel)
+        return dot(ref[...], sel)
 
     def part(g):
         return pl.ds(pl.multiple_of(g * own, own), own)
 
     def spread_rows(sel):
-        extra = dot(rows_s[...], sel)
+        extra = dot(rows_s[...], sel[:heads])
         return [extra[2 * i : 2 * i + 1] + extra[2 * i + 1 : 2 * i + 2] for i in range(7)]
 
     def chain(src, dst, ssem, rsem, g, to):
@@ -199,9 +204,7 @@
         mid, _, _, _, _, after_g, whole_g = spread_rows(sel)
         w = (spread(into_s, sel) * x[:, part(g)].astype(f32)).astype(bf16)
         weighted[:, part(g)] = w
-        state = mid * lax.dot_general(
-            last_b[...], w, (((0,), (0,)), ((), ())), preferred_element_type=f32
-        )
+        state = mid * dot(last_b[...], w)
         state_s[g] = state
 
         @pl.when(has_prev)
@@ -307,10 +310,10 @@
     backs = doc_ids.reshape(n_head, tokens)[:, -1].astype(f32)
     backs = jnp.broadcast_to(jnp.pad(backs, (0, tall - n_head))[:, None], (tall, 128))
     vmem = pl.BlockSpec(memory_space=pltpu.VMEM)
-    hbm = pl.BlockSpec(memory_space=pl.ANY)
+    hbm = pl.BlockSpec(memory_space=pltpu.HBM)
     dma = pltpu.SemaphoreType.DMA
     travel = pltpu.VMEM((chunks, STATE, WIDTH), bf16)
-    pair = pltpu.VMEM((2, tokens, heads), bf16)
+    pair = pltpu.VMEM((tokens, 2 * heads), bf16)
     gated, scale = pl.pallas_call(
         functools.partial(kernel, n_ctx, n_head, chunks, LAG),
         out_shape=(
@@ -324,7 +327,7 @@
             pltpu.VMEM((tokens, columns), bf16),
             pair, pair, pair,
             pltpu.VMEM((tokens, tokens), bf16),
-            pltpu.VMEM((tokens, STATE), bf16),
+            pltpu.VMEM((STATE, tokens), bf16),
             pltpu.VMEM((tokens, STATE), bf16),
             pltpu.VMEM((EXTRA, heads), bf16),
             pltpu.VMEM((n_head, 8, 128), f32),
@@ -337,9 +340,12 @@
             dma((2,)), dma((n_head,)), dma((n_head,)), dma((n_head,)), dma((n_head,)), dma((2,)),
         ]
         + [dma((chunks,))] * 6
-        + [pltpu.VMEM((tokens, columns), bf16)],
+        + [
+            pltpu.VMEM((tokens, columns), bf16),
+            pltpu.VMEM((chunks, 2 * heads, WIDTH), bf16),
+        ],
         compiler_params=pltpu.CompilerParams(
-            collective_id=0, has_side_effects=True, vmem_limit_bytes=44 * 2**20
+            collective_id=0, has_side_effects=True, vmem_limit_bytes=49 * 2**20
         ),
         cost_estimate=pl.CostEstimate(
             flops=3 * 10**9, bytes_accessed=10**7, transcendentals=2 * 10**6

time: 66.1 us -> 58 us (0.88); the launches traced: 64.9 us -> 57.7 us
  local copies, waits for them, and re-layouts: 7.53 us -> 3.75 us
  Pallas kernels: 53.7 us -> 50.3 us
    unnamed x9 -> x5, local copies, waits for them, and re-layouts: 5.62 us -> 1.84 us
    pallas_call x1, Pallas kernels: 53.7 us -> 50.3 us  [shards(): pl.pallas_call(functools.partial(kernel, n_ctx, n_head, chunks, LAG), out...]
where the time goes in v4:
time: 58 us; the launch traced here: 57.7 us
  Pallas kernels  50.3 us (87%)
  local copies, waits for them, and re-layouts  3.75 us (6%)
  other arithmetic  3.6 us (6%)
    pallas_call x1, Pallas kernels, shards(): pl.pallas_call(functools.partial(kernel, n_ctx, n_head, chunks, LAG), out...  50.3 us
    convert_element_type x1, other arithmetic, shards(): return (gated.astype(f32) * scale[:, :1] * norm_gain[None, :]).astype(bf16)  2.71 us
    unnamed x5, local copies, waits for them, and re-layouts  1.84 us

profile of v4, /device:TPU:5, one launch (start us, length us, event | category | flops | bytes accessed | tf_op | source)
XLA Modules:
  0.0 57.7 jit_solution(1930984391242272055)
XLA Ops:
  0.0 0.8 %dynamic_slice.3 = s32[384]{0:T(512)S(1)} dynamic-slice(s32[1536]{0:T(1024)} %param.13, s32[]{:T(128)S(6)} %select_n.16), dynamic_slice_sizes={384} | dynamic-slice | bytes 3076 | tf_op jit(solution)/shard_map/dynamic_slice | solution.py:303
  0.8 0.7 %pad_maximum_fusion = f32[3,16]{1,0:T(4,128)S(1)} fusion(f32[1,16]{1,0:T(1,128)} %bitcast.3, f32[1,16]{1,0:T(1,128)} %bitcast.4, f32[1,16]{1,0:T(1,128)} %bitcast.5), kind=kLoop, calls=%fused_computation.4 | loop fusion | flops 96 | bytes 384 | tf_op jit(solution)/shard_map/stack | solution.py:304
  1.5 0.1 tile.10
  1.6 0.7 %reshape.24 = s32[4,384]{1,0:T(4,128)S(1)} reshape(s32[1536]{0:T(1024)} %param.13) | data formatting | bytes 12288 | tf_op jit(solution)/shard_map/reshape | solution.py:310
  2.3 0.2 fusion
  2.5 0.1 broadcast_in_dim.30.backs
  2.6 0.9 %copy.13.dt_raw = bf16[384,64]{1,0:T(8,128)(2,1)S(1)} copy(bf16[384,64]{0,1:T(8,128)(2,1)} %param.12) | data formatting | bytes 98304 | tf_op args[3]
  3.5 0.1 broadcast_in_dim.31.ids_col
  3.6 0.0 copy-start
  3.6 0.9 %copy-done = bf16[384,256]{1,0:T(8,128)(2,1)S(1)} copy-done((bf16[384,256]{1,0:T(8,128)(2,1)S(1)}, bf16[384,256]{1,0:T(8,128)(2,1)}, u32[]{:S(2)}) %copy-start) | copy-done | bytes 196632
  4.5 0.0 copy-start.1
  4.5 50.3 %shard_map.91 = (bf16[384,4096]{1,0:T(8,128)(2,1)S(1)}, f32[384,128]{1,0:T(8,128)S(1)}) custom-call(bf16[384,4096]{1,0:T(8,128)(2,1)} %x_hbm.1, bf16[384,4096]{1,0:T(8,128)(2,1)} %gate_hbm.1, bf16[384,256]{1,0:T(8,128)(2,1)S(1)} %copy-done, bf16[384,64]{1,0:T(8,128)(2,1)S(1)} %copy.13.dt_raw, s32[384,1]{1,0:T(8,128)S(1)} %broadcast_in_dim.31.ids_col, ...), custom_call_target="tpu_custom_call" | custom-call | flops 3000000000 | bytes 10000000 | tf_op jit(solution)/shard_map/pallas_call | solution.py:317
  54.8 0.1 slice_reduce_fusion
  55.0 0.0 copy-done.1
  55.0 2.7 %multiply_convert_fusion = bf16[384,4096]{1,0:T(8,128)(2,1)} fusion(bf16[384,4096]{1,0:T(8,128)(2,1)S(1)} %get-tuple-element.7, f32[4096]{0:T(1024)S(1)} %copy-done.1, f32[384]{0:T(512)S(1)} %slice_reduce_fusion), kind=kLoop, calls=%fused_computation | loop fusion | flops 6291456 | bytes 6309376 | tf_op jit(solution)/shard_map/convert_element_type | solution.py:354
  (6 shorter events, 0.0 us)
Async XLA Ops:
  3.6 0.9 %copy-start = (bf16[384,256]{1,0:T(8,128)(2,1)S(1)}, bf16[384,256]{1,0:T(8,128)(2,1)}, u32[]{:S(2)}) copy-start(bf16[384,256]{1,0:T(8,128)(2,1)} %bc.1) | copy-start | bytes 589828
  4.5 50.5 %copy-start.1 = (f32[4096]{0:T(1024)S(1)}, f32[4096]{0:T(1024)}, u32[]{:S(2)}) copy-start(f32[4096]{0:T(1024)} %param.17) | copy-start | bytes 49156
